TPU v7x, 256 devices: a whole 4x4x8 slice. The times are simulated.
256 devices in a mesh: dp: 32 (over x, y, core), ctx: 8 (over z).
Axes of the slice: x: 4, y: 4, z: 8, core: 2. Of those that a mesh axis runs over, the one named last changes fastest.
Arguments:
- embedded: bfloat16 [8, 6144, 1024], P('ctx', 'dp'), may hold values from -30 to 30
- upstream: bfloat16 [8, 6144, 1024], P('ctx', 'dp'), may hold values from -6 to 6
- w_uvqk: bfloat16 [1024, 2048], replicated, may hold values from -0.1875 to 0.1875
- w_out: bfloat16 [512, 1024], replicated, may hold values from -0.25 to 0.25
- lengths: int32 [64], replicated, may hold values from 1 to 31, as said below
Outputs:
- layer_out: bfloat16 [8, 6144, 1024], P('ctx', 'dp')
- embedded_gradient: bfloat16 [8, 6144, 1024], P('ctx', 'dp')
- grad_w_uvqk: float32 [1024, 2048], P('ctx', 'dp')
- grad_w_out: float32 [512, 1024], P('ctx', 'dp')
Inputs may be any that keep to these rules, and one draw needn't show every extreme that they name: The 2 sequences of one owner hold at most 32 blocks together; in every draw some owner holds exactly 32; the lengths sum to 512.
All inputs are finite; a program needn't handle non-finite values.
Results may differ from a plain program's by a relative error of at most 0.025.
Values may be sent and summed in bfloat16 or wider, within the bound.
A program may use at most 128 MiB of HBM per device.

v0:
```python
import functools
import math

import jax
import jax.numpy as jnp
import numpy as np
from jax import lax
from jax.experimental import pallas as pl
from jax.experimental.pallas import tpu as pltpu
from jax.sharding import PartitionSpec as P

HEAD_DIM = 64
BR = 12
SEQ_DP = 2
GROUP = 4
LANES = 128
EPS = 1e-06
BIG = 1e30
MESH = pl.DeviceIdType.MESH
BF = jnp.bfloat16
F32 = jnp.float32
VMEM = pl.BlockSpec(memory_space=pltpu.VMEM)
SMEM = pl.BlockSpec(memory_space=pltpu.SMEM)
HBM = pl.BlockSpec(memory_space=pltpu.HBM)
LIMIT = 62 * 1024 * 1024
PIECES = 3
OUT = (3, 2, 1)
PREPARED = True
TILES = 30
BACK = (3, 1, 2)


class Cfg:
    def __init__(self, n_dp, n_ctx, rows, width):
        self.n_dp = n_dp
        self.n_ctx = n_ctx
        self.rows = rows
        self.width = width
        self.blocks = rows // BR
        self.heads = n_ctx
        self.hd = self.heads * HEAD_DIM
        self.half = n_ctx // 2
        self.piece_z = rows // 2
        self.piece_c = n_ctx * BR // 2
        self.span = n_dp * BR
        self.side = math.isqrt(n_dp // 2)
        self.total = n_ctx * self.span
        self.tile = min(512, self.total // 3)
        self.tab_owner = n_dp
        self.tab_own = n_dp + self.blocks + 1


def permutation(contexts):
    size = contexts * GROUP * BR
    matrix = np.zeros((size, size), np.float32)
    for block in range(GROUP):
        for context in range(contexts):
            for row in range(BR):
                matrix[
                    (block * contexts + context) * BR + row, (context * GROUP + block) * BR + row
                ] = 1.0
    return matrix


def lane(shape):
    return lax.broadcasted_iota(jnp.int32, shape, len(shape) - 1)


def swap(tensor):
    return pltpu.roll(tensor, HEAD_DIM, 1)


def join(left, right):
    return jnp.where(lane(left.shape) < HEAD_DIM, left, right)


def mm(left, right):
    return jnp.dot(left, right, preferred_element_type=F32)


def mm_nt(left, right):
    return lax.dot_general(left, right, (((1,), (1,)), ((), ())), preferred_element_type=F32)


def layer_normalize(tensor):
    centre = jnp.mean(tensor, -1, keepdims=True)
    centred = tensor - centre
    inverse = lax.rsqrt(jnp.mean(centred * centred, -1, keepdims=True) + EPS)
    return centred * inverse, inverse


def layer_norm_backward(incoming, normal, inverse):
    first = jnp.mean(incoming, -1, keepdims=True)
    second = jnp.mean(incoming * normal, -1, keepdims=True)
    return (incoming - first - normal * second) * inverse


def silu(argument):
    return argument * jax.nn.sigmoid(argument)


def silu_grad(argument):
    sigmoid = jax.nn.sigmoid(argument)
    return sigmoid * (1.0 + argument * (1.0 - sigmoid))


def pack_rows(value):
    mid = value.shape[0] // 2
    top, low = value[:mid], value[mid:]
    return join(top, swap(low)), join(swap(top), low)


def unpack_rows(first, second):
    first, second = first.astype(F32), second.astype(F32)
    return jnp.concatenate([join(first, swap(second)), join(swap(first), second)], axis=0)


def greet(cfg, me, ctx):
    barrier = pltpu.get_barrier_semaphore()

    def along_dp(k, carry):
        pl.semaphore_signal(
            barrier, inc=1, device_id={"dp": lax.rem(me + k, cfg.n_dp)}, device_id_type=MESH
        )
        return carry

    def along_ctx(k, carry):
        pl.semaphore_signal(
            barrier, inc=1, device_id={"ctx": lax.rem(ctx + k, cfg.n_ctx)}, device_id_type=MESH
        )
        return carry

    lax.fori_loop(1, cfg.n_dp, along_dp, 0)
    lax.fori_loop(1, cfg.n_ctx, along_ctx, 0)
    return barrier, cfg.n_dp + cfg.n_ctx - 2


class Part:
    def __init__(self, ref, *prefix):
        self.ref, self.prefix = ref, prefix

    def whole(self, index):
        return (*self.prefix, *(index if isinstance(index, tuple) else (index,)))

    def at(self, index):
        return self.ref.at[self.whole(index)]

    def __getitem__(self, index):
        return self.ref[self.whole(index)]

    def __setitem__(self, index, value):
        self.ref[self.whole(index)] = value


class Exchange:
    def __init__(self, axis, count, mine, source, target, send_sem, recv_sem):
        self.axis, self.count, self.mine = axis, count, mine
        self.source, self.target = source, target
        self.send_sem, self.recv_sem = send_sem, recv_sem

    def copy(self, other, slot):
        return pltpu.make_async_remote_copy(
            src_ref=self.source.at(other),
            dst_ref=self.target.at(slot),
            send_sem=self.send_sem.at(other),
            recv_sem=self.recv_sem.at(slot),
            device_id={self.axis: other},
            device_id_type=MESH,
        )

    def each(self, act):
        def step(k, carry):
            act(lax.rem(self.mine + k, self.count))
            return carry

        lax.fori_loop(1, self.count, step, 0)

    def start(self, before=None):
        def act(other):
            if before is not None:
                before(other)
            self.copy(other, self.mine).start()

        self.each(act)

    def wait_recv(self):
        self.each(lambda other: self.copy(other, other).wait_recv())

    def wait_send(self):
        self.each(lambda other: self.copy(other, self.mine).wait_send())


def regroup_in(cfg, g, source, perm, chunks):
    half_blocks = cfg.blocks // 2
    yl, yr = (
        mm(perm[...], jnp.concatenate([source(i) for i in range(lo, lo + cfg.half)], axis=0))
        for lo in (0, cfg.half)
    )
    left = join(yl, swap(yr)).astype(BF)
    right = join(swap(yl), yr).astype(BF)
    for b in range(GROUP):
        rows = slice(b * cfg.piece_c, (b + 1) * cfg.piece_c)
        chunks[GROUP * g + b] = left[rows]
        chunks[half_blocks + GROUP * g + b] = right[rows]


def regroup_out(cfg, g, picked, perm_t, store):
    width = GROUP * BR
    yl, yr = (
        mm(
            perm_t[...],
            jnp.concatenate([picked(lo + GROUP * g + b) for b in range(GROUP)], axis=0),
        )
        for lo in (0, cfg.blocks // 2)
    )
    left = join(yl, swap(yr)).astype(BF)
    right = join(swap(yl), yr).astype(BF)
    for i in range(cfg.half):
        rows = slice(width * i, width * (i + 1))
        store(i, left[rows])
        store(cfg.half + i, right[rows])


def unstream(cfg, own, piece, perm_t, store):
    width = GROUP * BR
    for g in range(cfg.n_dp // GROUP):
        rows = [piece[lax.rem(own + GROUP * g + b, cfg.n_dp)] for b in range(GROUP)]
        straight = mm(perm_t[...], jnp.concatenate(rows, axis=0))
        turned = swap(straight)
        for i in range(cfg.half):
            cut = slice(width * i, width * (i + 1))
            for c, one, two in ((i, straight, turned), (cfg.half + i, turned, straight)):
                at = cfg.span * c + width * g
                store(slice(at, at + width), g, one[cut], two[cut])


def to_stream(cfg, source, perm, stream, in_right):
    width = GROUP * BR
    for g in range(cfg.n_dp // GROUP):
        xl, xr = (
            jnp.concatenate(
                [
                    source[cfg.span * i + width * g : cfg.span * i + width * (g + 1)]
                    for i in range(lo, lo + cfg.half)
                ],
                axis=0,
            )
            for lo in (0, cfg.half)
        )
        both = join(swap(xl), xr) if in_right else join(xl, swap(xr))
        y = mm(perm[...], both.astype(BF)).astype(BF)
        for b in range(GROUP):
            stream[GROUP * g + b] = y[b * cfg.piece_c : (b + 1) * cfg.piece_c]


def dma(*shape):
    return pltpu.SemaphoreType.DMA(shape)


def params(collective):
    return pltpu.CompilerParams(
        collective_id=collective, has_side_effects=True, vmem_limit_bytes=LIMIT
    )


def table(cfg, me, lengths, tab):
    n = cfg.n_dp
    wrap = n * cfg.blocks * n

    def owner(o, carry):
        start, own, own_first, own_total, owners = carry
        first = lengths[SEQ_DP * o]
        total = first + lengths[SEQ_DP * o + 1]
        block = start + lax.rem(me - start + wrap, n)
        tab[o] = jnp.clip((block - me) // n, 0, cfg.blocks - 1)
        mine = o == me
        own = jnp.where(mine, start, own)
        own_first = jnp.where(mine, first, own_first)
        own_total = jnp.where(mine, total, own_total)
        owners = tuple(
            count + jnp.where(start <= me + n * j, 1, 0) for j, count in enumerate(owners)
        )
        return start + total, own, own_first, own_total, owners

    zero = jnp.int32(0)
    _, own, first, total, owners = lax.fori_loop(
        0, n, owner, (zero, zero, zero, zero, (jnp.int32(-1),) * cfg.blocks)
    )
    for j, count in enumerate(owners):
        tab[cfg.tab_owner + j] = count
    tab[cfg.tab_own] = lax.rem(own, n)
    tab[cfg.tab_own + 1] = first * BR
    tab[cfg.tab_own + 2] = total * BR


def segments(cfg, tab):
    shape = (cfg.span, LANES)
    inside = lax.broadcasted_iota(jnp.int32, shape, 0)
    first, total = tab[cfg.tab_own + 1], tab[cfg.tab_own + 2]
    segment = jnp.where(inside < first, 0, jnp.where(inside < total, 1, 2))
    which = lane(shape)
    seg_q = jnp.where(which == segment, -BIG, 0.0)
    seg_k = jnp.where((which < 3) & (which != segment), 1.0, 0.0)
    return seg_q, seg_k


def pack_out_term(cfg, term, t_out):
    side = cfg.side
    for tile in range(cfg.width // LANES):
        straight = term[:, tile * LANES : (tile + 1) * LANES]
        turned = swap(straight)
        for c in range(cfg.n_ctx):
            at = c * HEAD_DIM
            mid, end = at + HEAD_DIM // 2, at + HEAD_DIM
            pieces = (
                join(straight[at:mid], turned[mid:end]),
                join(turned[at:mid], straight[mid:end]),
            )
            for odd, piece in enumerate(pieces):
                s, t = divmod(2 * tile + odd, side)
                place = (0, t, s) if c < cfg.half else (1, (s + t) % side, s)
                t_out[(*place, c % cfg.half)] = piece.astype(BF)


def triangle(cfg, axis):
    shape = (cfg.tile, cfg.tile)
    query = lax.broadcasted_iota(jnp.int32, shape, axis)
    return lax.broadcasted_iota(jnp.int32, shape, 1 - axis) > query


def span_of(cfg, index):
    return slice(index * cfg.tile, (index + 1) * cfg.tile)


def at_tile(cfg, index):
    return pl.ds(pl.multiple_of(index * cfg.tile, cfg.tile), cfg.tile)


def attend(cfg, vk, qs, keys, att):
    each = cfg.total // cfg.tile
    half = each // 2

    def pair(i, j, diagonal):
        it, jt = at_tile(cfg, i), at_tile(cfg, j)
        h = mm_nt(qs[it], keys[jt])
        if diagonal:
            h = jnp.where(triangle(cfg, 0), -BIG, h)
        step = mm((h + h * jnp.tanh(h)).astype(BF), vk[jt])
        att[it] = step if diagonal else att[it] + step

    def diagonal(k, carry):
        for p in range(half):
            pair(half * k + p, half * k + p, True)
        return carry

    def round_of(k, carry):
        for i, j in round_pairs(cfg, k):
            pair(i, j, False)
        return carry

    lax.fori_loop(0, 2, diagonal, 0)
    lax.fori_loop(0, each - 1, round_of, 0)


def weigh_back(cfg, qs, keys, i, j, diagonal):
    h = mm_nt(keys[at_tile(cfg, j)], qs[at_tile(cfg, i)])
    if diagonal:
        h = jnp.where(triangle(cfg, 1), -BIG, h)
    p = 1.0 + jnp.tanh(h)
    a = h * p
    return a.astype(BF), p * ((2.0 * h + 1.0) - a)


def round_pairs(cfg, k):
    last = cfg.total // cfg.tile - 1
    pairs = [(last, k)]
    for d in range(1, (last + 1) // 2):
        one, two = lax.rem(k + d, last), lax.rem(k - d + last, last)
        pairs.append((jnp.maximum(one, two), jnp.minimum(one, two)))
    return pairs


def prepare(cfg, qs, keys, tiles, rounds):
    each = cfg.total // cfg.tile

    def one(k, carry):
        for p, (i, j) in enumerate(round_pairs(cfg, k)):
            weights, slope = weigh_back(cfg, qs, keys, i, j, False)
            tiles[each * k + 2 * p] = weights
            tiles[each * k + 2 * p + 1] = slope.astype(BF)
        return carry

    lax.fori_loop(*rounds, one, 0)


def attend_back(cfg, vk, vkt, qs, keys, go, qz, dvk, dqt, tiles):
    each = cfg.total // cfg.tile
    half = each // 2

    def pair(i, j, weights, slope, first):
        it, jt = at_tile(cfg, i), at_tile(cfg, j)
        grad_s = (mm_nt(vk[jt], go[it]) * slope).astype(BF)
        query = mm(vkt[:, jt], grad_s)
        key = mm(
            jnp.concatenate([weights, grad_s], axis=1),
            jnp.concatenate([go[it], qz[it]], axis=0),
        )
        dqt[:, it] = query if first else dqt[:, it] + query
        dvk[jt] = key if first else dvk[jt] + key

    def diagonal(k, carry):
        for p in range(half):
            i = half * k + p
            pair(i, i, *weigh_back(cfg, qs, keys, i, i, True), True)
        return carry

    def round_of(k, carry):
        for p, (i, j) in enumerate(round_pairs(cfg, k)):
            if PREPARED:
                weights = tiles[each * k + 2 * p]
                slope = tiles[each * k + 2 * p + 1].astype(F32)
            else:
                weights, slope = weigh_back(cfg, qs, keys, i, j, False)
            pair(i, j, weights, slope, False)
        return carry

    lax.fori_loop(0, 2, diagonal, 0)
    lax.fori_loop(0, each - 1, round_of, 0)


def scratch(cfg):
    side, half, block, count = cfg.side, cfg.half, cfg.width // cfg.n_ctx, PIECES
    deep, line, tiles, groups = block + 32, 2 * cfg.side, cfg.hd // LANES, cfg.blocks // 2 // GROUP
    chunk = (cfg.piece_c, LANES)
    zpart = (cfg.piece_z, LANES)
    zhalf = (groups, cfg.n_ctx, cfg.piece_z // groups, LANES)
    stream = (cfg.total, LANES)
    buffers = {
        "xv": ((cfg.rows, cfg.width), BF),
        "upv": ((cfg.rows, cfg.width), BF),
        "wv": ((cfg.width, 4 * cfg.hd), BF),
        "wov": ((cfg.hd, cfg.width), BF),
        "pre": ((cfg.rows, 4 * cfg.hd), F32),
        "normed": ((2, cfg.rows, cfg.width // 2), BF),
        "zsend0": ((count, cfg.n_ctx, *zpart), BF),
        "zland0": ((count, cfg.n_ctx, *zpart), BF),
        "chunks": ((count, cfg.blocks, *chunk), BF),
        "send0": ((count, cfg.n_dp, *chunk), BF),
        "land00": ((cfg.n_dp, *chunk), BF),
        "land01": ((cfg.n_dp, *chunk), BF),
        "land02": ((cfg.n_dp, *chunk), BF),
        "vk": (stream, BF),
        "qs": (stream, BF),
        "keys": (stream, BF),
        "qz": (stream, BF),
        "go": (stream, BF),
        "rows32": (stream, F32),
        "dqt": ((LANES, cfg.total), F32),
        "stream": ((count, cfg.n_dp, *chunk), BF),
        "send1": ((cfg.n_dp, *chunk), BF),
        "land1": ((cfg.n_dp, *chunk), BF),
        "zsend1": (zhalf, BF),
        "zland1": (zhalf, BF),
        "zsend2": (zhalf, BF),
        "zland2": (zhalf, BF),
        "chunks2": ((cfg.blocks, *chunk), BF),
        "send2": ((cfg.n_dp, *chunk), BF),
        "land2": ((cfg.n_dp, *chunk), BF),
        "att_norm": ((cfg.rows, cfg.hd), F32),
        "gpu": ((tiles, cfg.rows, LANES), BF),
        "t_out": ((2, side, side, half, 32, LANES), BF),
        "send3": ((count, cfg.n_dp, *chunk), BF),
        "land30": ((cfg.n_dp, *chunk), BF),
        "land31": ((cfg.n_dp, *chunk), BF),
        "land32": ((cfg.n_dp, *chunk), BF),
        "zsend3": ((count, cfg.n_ctx, *zpart), BF),
        "zland3": ((count, cfg.n_ctx, *zpart), BF),
        "gp": ((cfg.rows, 4 * cfg.hd), BF),
        "gpt": ((count, tiles, cfg.rows, LANES), BF),
        "lrecv": ((line, cfg.rows, cfg.width // 2), BF),
        "grecv": ((side, line, cfg.rows, LANES), BF),
        "trecv": ((line, side, half, 32, LANES), BF),
        "normal_t": ((cfg.width // 2, line * cfg.rows), BF),
        "bsend": ((side, half, block, LANES), BF),
        "brecv": ((side, half, block, LANES), BF),
        "acc": ((half, deep, LANES), F32),
        "tiles": ((TILES, cfg.tile, cfg.tile), BF),
        "vkt": ((LANES, cfg.total), BF),
        "bsend_o": ((side, half, 32, LANES), BF),
        "brecv_o": ((side, half, 32, LANES), BF),
        "fsend": ((half, 2, deep // 2, LANES), BF),
        "frecv": ((cfg.n_ctx, deep // 2, LANES), BF),
    }
    sems = {
        "in": (7,),
        "ls": (6, line - 1),
        "lr": (6, line),
        "bs": (2, side),
        "br": (2, side),
        "fs": (half, 2),
        "fr": (cfg.n_ctx,),
    }
    for name, size, parts in (
        ("z0", cfg.n_ctx, count),
        ("x0", cfg.n_dp, count),
        ("x1", cfg.n_dp, 1),
        ("z1", cfg.n_ctx, groups),
        ("z2", cfg.n_ctx, groups),
        ("x2", cfg.n_dp, 1),
        ("x3", cfg.n_dp, count),
        ("z3", cfg.n_ctx, count),
    ):
        sems[name + "s"] = (parts, size)
        sems[name + "r"] = (parts, size)
    shapes = {name: pltpu.VMEM(*spec) for name, spec in buffers.items()}
    shapes["tab"] = pltpu.SMEM((cfg.tab_own + 3,), jnp.int32)
    shapes.update({name: dma(*size) for name, size in sems.items()})
    return shapes


def layer_kernel(cfg, names, *refs):
    r = dict(zip(names, refs))
    perm, perm_t, tab = r["perm"], r["perm_t"], r["tab"]
    hd, rows, side, half, n, n_ctx = cfg.hd, cfg.rows, cfg.side, cfg.half, cfg.n_dp, cfg.n_ctx
    count, width, groups = PIECES, GROUP * BR, cfg.blocks // 2 // GROUP
    me, ctx = lax.axis_index("dp"), lax.axis_index("ctx")
    core = lax.rem(me, 2)
    other = 1 - core
    chip_x, chip_y = me // (2 * side), lax.rem(me // 2, side)
    a_own = chip_x * other + chip_y * core
    b_own = chip_y * other + chip_x * core
    along_a = 2 * side - core * (2 * side - 2)
    along_b = 2 + core * (2 * side - 2)
    home = ctx // half
    m_own = 2 * a_own + core

    def device(a, b):
        return a * along_a + b * along_b + core

    adder = (chip_y * side + lax.rem(chip_x + chip_y, side)) * 2 + home
    s_own = lax.rem(chip_y - chip_x + side, side)
    owner = (s_own * side + chip_x) * 2

    def load(number, source, target):
        return pltpu.make_async_copy(source, target, r["in"].at[number])

    loads = [load(0, r["x"].at[0], r["xv"])]
    for i, s in enumerate((*OUT, 0)):
        cut = pl.ds(s * hd, hd)
        loads.append(load(1 + i, r["w"].at[:, cut], r["wv"].at[:, cut]))
    loads.append(load(5, r["up"].at[0], r["upv"]))
    loads.append(load(6, r["w_out"], r["wov"]))
    for item in loads:
        item.start()

    barrier, greetings = greet(cfg, me, ctx)
    for z in range(n_ctx):

        @pl.when(jnp.logical_or(z != ctx, adder != me))
        def _():
            pl.semaphore_signal(
                barrier, inc=1, device_id={"dp": adder, "ctx": z}, device_id_type=MESH
            )

    table(cfg, me, r["lengths"], tab)
    own = tab[cfg.tab_own]

    def moves(axis, source, target, sems, parts):
        size, mine = (n, me) if axis == "dp" else (n_ctx, ctx)
        return [
            Exchange(
                axis,
                size,
                mine,
                source(t),
                target(t),
                Part(r[sems + "s"], t),
                Part(r[sems + "r"], t),
            )
            for t in range(parts)
        ]

    def part(name):
        return lambda t: Part(r[name], t)

    z0 = moves("ctx", part("zsend0"), part("zland0"), "z0", count)
    x0 = moves("dp", part("send0"), lambda t: Part(r["land0" + str(t)]), "x0", count)
    x1 = moves("dp", lambda t: Part(r["send1"]), lambda t: Part(r["land1"]), "x1", 1)[0]
    z1 = moves("ctx", part("zsend1"), part("zland1"), "z1", groups)
    z2 = moves("ctx", part("zsend2"), part("zland2"), "z2", groups)
    x2 = moves("dp", lambda t: Part(r["send2"]), lambda t: Part(r["land2"]), "x2", 1)[0]
    x3 = moves("dp", part("send3"), lambda t: Part(r["land3" + str(t)]), "x3", count)
    z3 = moves("ctx", part("zsend3"), part("zland3"), "z3", count)

    xv, upv, wv, wov, pre = r["xv"], r["upv"], r["wv"], r["wov"], r["pre"]
    normed_ref = r["normed"]
    loads[0].wait()
    normal, inverse = layer_normalize(xv[...].astype(F32))
    normed = normal.astype(BF)
    normed_ref[0] = normed[:, : cfg.width // 2]
    normed_ref[1] = normed[:, cfg.width // 2 :]
    zsend0, zland0, chunks, send0 = r["zsend0"], r["zland0"], r["chunks"], r["send0"]
    step = min(256, hd)

    def section(number, t):
        for base in range(0, hd, step):
            at = number * hd + base
            value = mm(normed, wv[:, at : at + step])
            pre[:, at : at + step] = value
            if t is None:
                continue
            act = silu(value)
            for tile in range(step // LANES):
                head = (base + tile * LANES) // HEAD_DIM
                one, two = pack_rows(act[:, tile * LANES : (tile + 1) * LANES])
                zsend0[t, head] = one.astype(BF)
                zsend0[t, head + 1] = two.astype(BF)

    for t, number in enumerate(OUT):
        loads[1 + t].wait()
        section(number, t)
        if t == 0:
            pl.semaphore_wait(
                barrier, greetings + n_ctx - jnp.where(adder == me, 1, 0).astype(jnp.int32)
            )
        z0[t].start()
        zland0[t, ctx] = zsend0[t, ctx]
    loads[4].wait()
    section(0, None)
    loads[5].wait()
    loads[6].wait()
    back_gated = mm_nt(upv[...], wov[...])
    gate = silu(pre[:, :hd]).astype(BF).astype(F32)
    for t in range(count):
        z0[t].wait_recv()
        for g in range(groups):
            cut = slice(width * g, width * (g + 1))
            regroup_in(
                cfg, g, lambda i, t=t, cut=cut: zland0[t, i, cut], perm, Part(chunks, t)
            )

        def fill(device_at, t=t):
            send0[t, device_at] = chunks[t, tab[device_at]]

        x0[t].start(fill)
        r["land0" + str(t)][me] = chunks[t, tab[me]]

    vk, qs, keys, qz, go = r["vk"], r["qs"], r["keys"], r["qz"], r["go"]
    seg_q, seg_k = segments(cfg, tab)

    def store_k(cut, g, straight, turned):
        keys[cut] = join(seg_k[width * g : width * (g + 1)], turned).astype(BF)

    def store_v(cut, g, straight, turned):
        vk[cut] = join(straight.astype(BF), keys[cut])

    def store_q(cut, g, straight, turned):
        value = turned * (0.5 * HEAD_DIM**-0.5)
        qs[cut] = join(seg_q[width * g : width * (g + 1)], value).astype(BF)
        qz[cut] = join(jnp.zeros_like(value), value).astype(BF)

    tiles = r["tiles"]
    for t, store in enumerate((store_k, store_q, store_v)):
        x0[t].wait_recv()
        unstream(cfg, own, r["land0" + str(t)], perm_t, store)

    gpu, t_out, gpt = r["gpu"], r["t_out"], r["gpt"]
    lrecv, grecv, trecv = r["lrecv"], r["grecv"], r["trecv"]
    def tile_of(a, kind, s):
        return lax.rem(a - s * kind + side, side)

    def line_copy(what, j):
        if j < side - 1:
            kind, a = 0, lax.rem(chip_x + 1 + j, side)
            target, slot = (a * side + chip_y) * 2, 2 * chip_x + core
        elif j < 2 * (side - 1):
            kind, a = 1, lax.rem(chip_y + 1 + j - (side - 1), side)
            target, slot = (chip_x * side + a) * 2 + 1, 2 * chip_y + core
        else:
            kind, a = other, b_own
            target, slot = me + 1 - 2 * core, 2 * b_own + core
        if what == 4:
            source, target_ref = normed_ref.at[kind], lrecv.at[slot]
        elif what == 5:
            source, target_ref = t_out.at[kind, a], trecv.at[slot]
        elif what == 0:
            source, target_ref = gpu.at[tile_of(a, kind, 0)], grecv.at[0, slot]
        else:
            source, target_ref = gpt.at[what - 1, tile_of(a, kind, what)], grecv.at[what, slot]
        return pltpu.make_async_remote_copy(
            src_ref=source,
            dst_ref=target_ref,
            send_sem=r["ls"].at[what, j],
            recv_sem=r["lr"].at[what, slot],
            device_id={"dp": target},
            device_id_type=MESH,
        )

    def line_start(what):
        for j in range(2 * side - 1):
            line_copy(what, j).start()

    def line_wait(what):
        ref = {4: lrecv, 5: trecv}.get(what, None)
        for i in range(1, 2 * side):
            slot = lax.rem(m_own + i, 2 * side)
            place = grecv.at[what, slot] if ref is None else ref.at[slot]
            pltpu.make_async_remote_copy(
                src_ref=place,
                dst_ref=place,
                send_sem=r["ls"].at[what, 0],
                recv_sem=r["lr"].at[what, slot],
                device_id={"dp": me + 1 - 2 * core},
                device_id_type=MESH,
            ).wait_recv()


    line_start(4)
    rows32 = r["rows32"]
    attend(cfg, vk, qs, keys, rows32)

    stream, send1, land1 = r["stream"], r["send1"], r["land1"]
    to_stream(cfg, rows32, perm, Part(stream, 0), False)

    def place(t, device_at):
        return stream[t, lax.rem(device_at - own + n, n)]

    def fill1(device_at):
        send1[device_at] = place(0, device_at)

    x1.start(fill1)
    land1[me] = place(0, me)
    backward_gate = back_gated * gate
    lrecv[m_own] = normed_ref[core]
    line_wait(4)
    normal_t = r["normal_t"]
    for i in range(side):
        pair = jnp.concatenate([lrecv[2 * i], lrecv[2 * i + 1]], axis=0)
        normal_t[:, 2 * rows * i : 2 * rows * (i + 1)] = pair.T

    prepare(cfg, qs, keys, tiles, (0, 3))
    vkt = r["vkt"]
    for i in range(cfg.total // cfg.tile):
        vkt[:, span_of(cfg, i)] = vk[span_of(cfg, i)].T
    x1.wait_recv()
    zsend1, zland1, zsend2, zland2 = r["zsend1"], r["zland1"], r["zsend2"], r["zland2"]
    for g in range(groups):

        def store1(i, value, g=g):
            zsend1[g, i] = value

        regroup_out(cfg, g, lambda block: land1[tab[cfg.tab_owner + block]], perm_t, store1)
        z1[g].start()
        zland1[g, ctx] = zsend1[g, ctx]
    att_norm = r["att_norm"]
    mid = rows // 2
    for g in range(groups):
        z1[g].wait_recv()
        att_rows = jnp.concatenate(
            [
                unpack_rows(zland1[g, head], zland1[g, head + 1])
                for head in range(0, cfg.heads, 2)
            ],
            axis=1,
        )
        norm_part, att_inverse = layer_normalize(att_rows)
        top, low = slice(width * g, width * (g + 1)), slice(mid + width * g, mid + width * (g + 1))
        att_norm[top] = norm_part[:width]
        att_norm[low] = norm_part[width:]
        incoming = jnp.concatenate([backward_gate[top], backward_gate[low]], axis=0)
        grad_att = layer_norm_backward(incoming, norm_part, att_inverse)
        for tile in range(hd // LANES):
            one, two = pack_rows(grad_att[:, tile * LANES : (tile + 1) * LANES])
            zsend2[g, 2 * tile] = one.astype(BF)
            zsend2[g, 2 * tile + 1] = two.astype(BF)
        z2[g].start()
        zland2[g, ctx] = zsend2[g, ctx]

    gated = (att_norm[...] * gate).astype(BF)
    r["out"][0] = (xv[...].astype(F32) + mm(gated, wov[...])).astype(BF)
    chunks2, send2, land2 = r["chunks2"], r["send2"], r["land2"]
    for g in range(groups):
        z2[g].wait_recv()
        regroup_in(cfg, g, lambda i, g=g: zland2[g, i], perm, chunks2)

    def fill2(device_at):
        send2[device_at] = chunks2[tab[device_at]]

    x2.start(fill2)
    land2[me] = chunks2[tab[me]]
    gp = r["gp"]
    grad_u = (back_gated * att_norm[...] * silu_grad(pre[:, :hd])).astype(BF)
    gp[:, :hd] = grad_u
    for tile in range(hd // LANES):
        gpu[tile] = grad_u[:, tile * LANES : (tile + 1) * LANES]
    pack_out_term(
        cfg,
        lax.dot_general(gated, upv[...], (((0,), (0,)), ((), ())), preferred_element_type=F32),
        t_out,
    )
    prepare(cfg, qs, keys, tiles, (3, 5))
    x2.wait_recv()

    def store_go(cut, g, straight, turned):
        go[cut] = join(straight, jnp.zeros_like(straight)).astype(BF)

    line_start(0)
    line_start(5)
    unstream(cfg, own, land2, perm_t, store_go)
    dqt = r["dqt"]
    attend_back(cfg, vk, vkt, qs, keys, go, qz, rows32, dqt, tiles)

    send3, zsend3, zland3 = r["send3"], r["zsend3"], r["zland3"]
    for t in range(count):
        if t == 2:
            for i in range(cfg.total // cfg.tile):
                cut = slice(cfg.tile * i, cfg.tile * (i + 1))
                rows32[cut] = dqt[:, cut].T * (0.5 * HEAD_DIM**-0.5)
        to_stream(cfg, rows32, perm, Part(stream, t), t != 1)

        def fill3(device_at, t=t):
            send3[t, device_at] = place(t, device_at)

        x3[t].start(fill3)
        r["land3" + str(t)][me] = place(t, me)

    send_b, recv_b, acc = r["bsend"], r["brecv"], r["acc"]
    block = cfg.width // n_ctx
    grecv[0, m_own] = gpu[tile_of(a_own, core, 0)]
    trecv[m_own] = t_out[core, a_own]
    line_wait(0)
    line_wait(5)

    def add_copy(part, s):
        b = lax.rem(a_own + s * (1 - 2 * core) + side, side)
        slot = lax.rem(b_own - b + 2 * side - 1, side)
        source, target = ((send_b, recv_b), (r["bsend_o"], r["brecv_o"]))[part]
        return b == b_own, pltpu.make_async_remote_copy(
            src_ref=source.at[s],
            dst_ref=target.at[slot],
            send_sem=r["bs"].at[part, s],
            recv_sem=r["br"].at[part, slot],
            device_id={"dp": device(a_own, b)},
            device_id_type=MESH,
        )

    def add_part(part, s, value):
        mine, copy = add_copy(part, s)

        @pl.when(mine)
        def _():
            if part == 0:
                acc[:, :block] = value
            else:
                acc[:, block:] = value

        @pl.when(jnp.logical_not(mine))
        def _():
            if part == 0:
                send_b[s] = value.astype(BF)
            else:
                r["bsend_o"][s] = value.astype(BF)
            copy.start()

    def add_section(s):
        value = mm(normal_t[...], grecv[s].reshape(2 * side * rows, LANES))
        add_part(0, s, value.reshape(half, block, LANES))

    for s in range(side):
        low = trecv[0, s].astype(F32)
        for m in range(1, 2 * side):
            low = low + trecv[m, s].astype(F32)
        add_part(1, s, low)
    add_section(0)
    for t in range(count):
        x3[t].wait_recv()
        land = r["land3" + str(t)]
        for g in range(groups):

            def store3(i, value, t=t, g=g):
                zsend3[t, i, width * g : width * (g + 1)] = value

            regroup_out(
                cfg, g, lambda b, land=land: land[tab[cfg.tab_owner + b]], perm_t, store3
            )
        z3[t].start()
        zland3[t, ctx] = zsend3[t, ctx]

    def give_section(t):
        s = BACK[t]
        z3[t].wait_recv()
        for head in range(0, cfg.heads, 2):
            tile = head // 2
            at = s * hd + tile * LANES
            cut = slice(at, at + LANES)
            value = unpack_rows(zland3[t, head], zland3[t, head + 1])
            value = (value * silu_grad(pre[:, cut])).astype(BF)
            gp[:, cut] = value
            gpt[s - 1, tile] = value
        line_start(s)
        grecv[s, m_own] = gpt[s - 1, tile_of(a_own, core, s)]

    back = mm_nt(gp[:, :hd], wv[:, :hd])
    give_section(0)
    back = back + mm_nt(gp[:, 3 * hd :], wv[:, 3 * hd :])
    give_section(1)
    line_wait(BACK[0])
    add_section(BACK[0])
    give_section(2)
    line_wait(BACK[1])
    add_section(BACK[1])
    back = back + mm_nt(gp[:, hd : 2 * hd], wv[:, hd : 2 * hd])

    back = back + mm_nt(gp[:, 2 * hd : 3 * hd], wv[:, 2 * hd : 3 * hd])
    r["gradient"][0] = (
        upv[...].astype(F32) + layer_norm_backward(back, normal, inverse)
    ).astype(BF)
    line_wait(BACK[2])
    add_section(BACK[2])

    total = acc[...]
    for slot in range(side - 1):
        for part, target in enumerate((recv_b, r["brecv_o"])):
            pltpu.make_async_remote_copy(
                src_ref=target.at[slot],
                dst_ref=target.at[slot],
                send_sem=r["bs"].at[part, 0],
                recv_sem=r["br"].at[part, slot],
                device_id={"dp": me + 1 - 2 * core},
                device_id_type=MESH,
            ).wait_recv()
        arrived = jnp.concatenate([recv_b[slot], r["brecv_o"][slot]], axis=1)
        total = total + arrived.astype(F32)

    fsend, frecv = r["fsend"], r["frecv"]
    quarter = lax.rem(lane((16, LANES)), HEAD_DIM) < 32
    for h in range(half):
        top, low = total[h, : block // 2], total[h, block // 2 : block]
        u, v = total[h, block : block + 16], total[h, block + 16 :]
        fsend[h, 0, : block // 2] = join(top, swap(low)).astype(BF)
        fsend[h, 1, : block // 2] = join(swap(top), low).astype(BF)
        fsend[h, 0, block // 2 :] = jnp.where(quarter, u, pltpu.roll(v, 32, 1)).astype(BF)
        fsend[h, 1, block // 2 :] = jnp.where(quarter, pltpu.roll(u, 96, 1), v).astype(BF)

    def last_copy(h, kind):
        return pltpu.make_async_remote_copy(
            src_ref=fsend.at[h, kind],
            dst_ref=frecv.at[ctx],
            send_sem=r["fs"].at[h, kind],
            recv_sem=r["fr"].at[ctx],
            device_id={"dp": owner + kind, "ctx": half * core + h},
            device_id_type=MESH,
        )

    def stays(h, kind):
        return jnp.logical_and(half * core + h == ctx, owner + kind == me)

    for h in range(half):
        for kind in range(2):

            @pl.when(stays(h, kind))
            def _():
                frecv[ctx] = fsend[h, kind]

            @pl.when(jnp.logical_not(stays(h, kind)))
            def _():
                last_copy(h, kind).start()

    for z in range(n_ctx):

        @pl.when(jnp.logical_or(z != ctx, adder != me))
        def _():
            pltpu.make_async_remote_copy(
                src_ref=fsend.at[0, 0],
                dst_ref=frecv.at[z],
                send_sem=r["fs"].at[0, 0],
                recv_sem=r["fr"].at[z],
                device_id={"dp": me + 1 - 2 * core},
                device_id_type=MESH,
            ).wait_recv()

    total = frecv[0].astype(F32)
    for z in range(1, n_ctx):
        total = total + frecv[z].astype(F32)
    r["last"][...] = total * (rows * n * n_ctx) ** -0.5

    for move in (*z0, *x0, x1, *z1, *z2, x2, *x3, *z3):
        move.wait_send()
    for what in range(6):
        for j in range(2 * side - 1):
            line_copy(what, j).wait_send()
    for part in range(2):
        for s in range(side):
            mine, copy = add_copy(part, s)

            @pl.when(jnp.logical_not(mine))
            def _():
                copy.wait_send()

    for h in range(half):
        for kind in range(2):

            @pl.when(jnp.logical_not(stays(h, kind)))
            def _():
                last_copy(h, kind).wait_send()


def layer(cfg, lengths, x, up, w, w_out, perm, perm_t):
    block = cfg.width // cfg.n_ctx
    inputs = {
        "lengths": SMEM,
        "x": HBM,
        "up": HBM,
        "w": HBM,
        "w_out": HBM,
        "perm": VMEM,
        "perm_t": VMEM,
    }
    outputs = {
        "out": jax.ShapeDtypeStruct(x.shape, BF),
        "gradient": jax.ShapeDtypeStruct(x.shape, BF),
        "last": jax.ShapeDtypeStruct((block // 2 + 16, LANES), F32),
    }
    shapes = scratch(cfg)
    return pl.pallas_call(
        functools.partial(layer_kernel, cfg, [*inputs, *outputs, *shapes]),
        name="layer",
        out_shape=tuple(outputs.values()),
        in_specs=list(inputs.values()),
        out_specs=(VMEM,) * len(outputs),
        scratch_shapes=list(shapes.values()),
        compiler_params=params(0),
    )(lengths, x, up, w, w_out, perm, perm_t)


def finish_kernel(half_block, last, out, gradient, gw, go, out_copy, gradient_copy):
    front, low = last[:half_block].T, last[half_block:].T
    gw[...] = jnp.concatenate([front[:HEAD_DIM], front[HEAD_DIM:]], axis=1)
    go[...] = jnp.concatenate([low[32 * i : 32 * (i + 1)] for i in range(4)], axis=1)
    out_copy[...] = out[...]
    gradient_copy[...] = gradient[...]


def finish(cfg, last, out, gradient):
    block = cfg.width // cfg.n_ctx
    return pl.pallas_call(
        functools.partial(finish_kernel, block // 2),
        name="finish",
        out_shape=(
            jax.ShapeDtypeStruct((HEAD_DIM, block), F32),
            jax.ShapeDtypeStruct((32, HEAD_DIM), F32),
            jax.ShapeDtypeStruct(out.shape, BF),
            jax.ShapeDtypeStruct(out.shape, BF),
        ),
        in_specs=[VMEM] * 3,
        out_specs=(VMEM,) * 4,
        compiler_params=pltpu.CompilerParams(vmem_limit_bytes=LIMIT),
    )(last, out, gradient)


def shards(n_dp, n_ctx, embedded, upstream, w_uvqk, w_out, lengths):
    cfg = Cfg(n_dp, n_ctx, embedded.shape[1], embedded.shape[2])
    matrix = permutation(cfg.half)
    perm, perm_t = jnp.asarray(matrix, BF), jnp.asarray(matrix.T, BF)
    out, gradient, last = layer(cfg, lengths, embedded, upstream, w_uvqk, w_out, perm, perm_t)
    grad_w, grad_out, out, gradient = finish(cfg, last, out, gradient)
    return out, gradient, grad_w.T, grad_out.T


def solution(mesh):
    return jax.shard_map(
        functools.partial(shards, mesh.shape["dp"], mesh.shape["ctx"]),
        mesh=mesh,
        in_specs=(P("ctx", "dp", None), P("ctx", "dp", None), P(), P(), P()),
        out_specs=(P("ctx", "dp", None), P("ctx", "dp", None), P("ctx", "dp"), P("ctx", "dp")),
        check_vma=False,
    )
```

profile of v0, /device:TPU:29, one launch (start us, length us, event | category | flops | bytes accessed | tf_op | source)
XLA Modules:
  0.0 153.2 jit_solution(6191041320440642958)
XLA Ops:
  0.6 150.4 %layer.1 = (bf16[1,192,1024]{2,1,0:T(8,128)(2,1)}, bf16[1,192,1024]{2,1,0:T(8,128)(2,1)}, f32[80,128]{1,0:T(8,128)}) custom-call(s32[64]{0:T(128)} %refs_0_.1, bf16[1,192,1024]{2,1,0:T(8,128)(2,1)} %refs_1_.1, bf16[1,192,1024]{2,1,0:T(8,128)(2,1)} %refs_2_.1, bf16[1024,2048]{1,0:T(8,128)(2,1)} %refs_3_.1, bf16[512,1024]{1,0:T(8,128)(2,1)} %refs_4_.1, ...), custom_call_target="tpu_custom_call" | custom-call | tf_op jit(solution)/shard_map/layer/pallas_call | solution.py:1025
  151.1 2.1 %finish.1 = (f32[64,128]{1,0:T(8,128)}, f32[32,64]{1,0:T(8,128)}, bf16[1,192,1024]{2,1,0:T(8,128)(2,1)}, bf16[1,192,1024]{2,1,0:T(8,128)(2,1)}) custom-call(f32[80,128]{1,0:T(8,128)} %get-tuple-element.11.last, bf16[1,192,1024]{2,1,0:T(8,128)(2,1)} %get-tuple-element.12.out, bf16[1,192,1024]{2,1,0:T(8,128)(2,1)} %get-tuple-element.13.gradient), custom_call_target="tpu_custom_call" | custom-call | tf_op jit(solution)/shard_map/finish/pallas_call | solution.py:1046
where the time goes:
time: 153 us
  Pallas kernels  153 us (100%)
    pallas_call x1, Pallas kernels, layer(): pl.pallas_call(functools.partial(layer_kernel, cfg, [*inputs, *outputs, *...  150 us

commit v1 on v0

--- a/solution.py
+++ b/solution.py
@@ -221,29 +221,40 @@
         store(cfg.half + i, right[rows])
 
 
-def unstream(cfg, own, piece, perm_t, store):
+def in_pairs(count, act):
+    def both(k, carry):
+        act(2 * k)
+        act(2 * k + 1)
+        return carry
+
+    lax.fori_loop(0, count // 2, both, 0)
+
+
+def group_rows(cfg, context, g):
+    return pl.ds(pl.multiple_of(cfg.span * context + GROUP * BR * g, GROUP * BR), GROUP * BR)
+
+
+def unstream(cfg, own, piece, perm_t, store, extra):
     width = GROUP * BR
-    for g in range(cfg.n_dp // GROUP):
+
+    def one(g):
         rows = [piece[lax.rem(own + GROUP * g + b, cfg.n_dp)] for b in range(GROUP)]
         straight = mm(perm_t[...], jnp.concatenate(rows, axis=0))
         turned = swap(straight)
+        given = extra(g)
         for i in range(cfg.half):
             cut = slice(width * i, width * (i + 1))
-            for c, one, two in ((i, straight, turned), (cfg.half + i, turned, straight)):
-                at = cfg.span * c + width * g
-                store(slice(at, at + width), g, one[cut], two[cut])
+            for c, first, second in ((i, straight, turned), (cfg.half + i, turned, straight)):
+                store(group_rows(cfg, c, g), given, first[cut], second[cut])
+
+    in_pairs(cfg.n_dp // GROUP, one)
 
 
 def to_stream(cfg, source, perm, stream, in_right):
-    width = GROUP * BR
-    for g in range(cfg.n_dp // GROUP):
+    def one(g):
         xl, xr = (
             jnp.concatenate(
-                [
-                    source[cfg.span * i + width * g : cfg.span * i + width * (g + 1)]
-                    for i in range(lo, lo + cfg.half)
-                ],
-                axis=0,
+                [source[group_rows(cfg, i, g)] for i in range(lo, lo + cfg.half)], axis=0
             )
             for lo in (0, cfg.half)
         )
@@ -251,6 +262,8 @@
         y = mm(perm[...], both.astype(BF)).astype(BF)
         for b in range(GROUP):
             stream[GROUP * g + b] = y[b * cfg.piece_c : (b + 1) * cfg.piece_c]
+
+    in_pairs(cfg.n_dp // GROUP, one)
 
 
 def dma(*shape):
@@ -293,9 +306,9 @@
     tab[cfg.tab_own + 2] = total * BR
 
 
-def segments(cfg, tab):
-    shape = (cfg.span, LANES)
-    inside = lax.broadcasted_iota(jnp.int32, shape, 0)
+def segments(cfg, tab, g):
+    shape = (GROUP * BR, LANES)
+    inside = lax.broadcasted_iota(jnp.int32, shape, 0) + GROUP * BR * g
     first, total = tab[cfg.tab_own + 1], tab[cfg.tab_own + 2]
     segment = jnp.where(inside < first, 0, jnp.where(inside < total, 1, 2))
     which = lane(shape)
@@ -646,23 +659,24 @@
         r["land0" + str(t)][me] = chunks[t, tab[me]]
 
     vk, qs, keys, qz, go = r["vk"], r["qs"], r["keys"], r["qz"], r["go"]
-    seg_q, seg_k = segments(cfg, tab)
-
-    def store_k(cut, g, straight, turned):
-        keys[cut] = join(seg_k[width * g : width * (g + 1)], turned).astype(BF)
-
-    def store_v(cut, g, straight, turned):
+
+    def store_k(cut, masks, straight, turned):
+        keys[cut] = join(masks[1], turned).astype(BF)
+
+    def store_v(cut, masks, straight, turned):
         vk[cut] = join(straight.astype(BF), keys[cut])
 
-    def store_q(cut, g, straight, turned):
+    def store_q(cut, masks, straight, turned):
         value = turned * (0.5 * HEAD_DIM**-0.5)
-        qs[cut] = join(seg_q[width * g : width * (g + 1)], value).astype(BF)
+        qs[cut] = join(masks[0], value).astype(BF)
         qz[cut] = join(jnp.zeros_like(value), value).astype(BF)
 
     tiles = r["tiles"]
     for t, store in enumerate((store_k, store_q, store_v)):
         x0[t].wait_recv()
-        unstream(cfg, own, r["land0" + str(t)], perm_t, store)
+        unstream(
+            cfg, own, r["land0" + str(t)], perm_t, store, lambda g: segments(cfg, tab, g)
+        )
 
     gpu, t_out, gpt = r["gpu"], r["t_out"], r["gpt"]
     lrecv, grecv, trecv = r["lrecv"], r["grecv"], r["trecv"]
@@ -801,12 +815,12 @@
     prepare(cfg, qs, keys, tiles, (3, 5))
     x2.wait_recv()
 
-    def store_go(cut, g, straight, turned):
+    def store_go(cut, masks, straight, turned):
         go[cut] = join(straight, jnp.zeros_like(straight)).astype(BF)
 
     line_start(0)
     line_start(5)
-    unstream(cfg, own, land2, perm_t, store_go)
+    unstream(cfg, own, land2, perm_t, store_go, lambda g: None)
     dqt = r["dqt"]
     attend_back(cfg, vk, vkt, qs, keys, go, qz, rows32, dqt, tiles)
 

time: 153 us -> 156 us (1.020); the launches traced: 153 us -> 154 us
  no operation moved by 1% of the time
where the time goes in v1:
time: 156 us; the launch traced here: 154 us
  Pallas kernels  154 us (99%)
    pallas_call x1, Pallas kernels, layer(): pl.pallas_call(functools.partial(layer_kernel, cfg, [*inputs, *outputs, *...  152 us

profile of v1, /device:TPU:29, one launch (start us, length us, event | category | flops | bytes accessed | tf_op | source)
XLA Modules:
  0.0 154.4 jit_solution(5850757650023589931)
XLA Ops:
  0.6 151.7 %layer.1 = (bf16[1,192,1024]{2,1,0:T(8,128)(2,1)}, bf16[1,192,1024]{2,1,0:T(8,128)(2,1)}, f32[80,128]{1,0:T(8,128)}) custom-call(s32[64]{0:T(128)} %refs_0_.1, bf16[1,192,1024]{2,1,0:T(8,128)(2,1)} %refs_1_.1, bf16[1,192,1024]{2,1,0:T(8,128)(2,1)} %refs_2_.1, bf16[1024,2048]{1,0:T(8,128)(2,1)} %refs_3_.1, bf16[512,1024]{1,0:T(8,128)(2,1)} %refs_4_.1, ...), custom_call_target="tpu_custom_call" | custom-call | tf_op jit(solution)/shard_map/layer/pallas_call | solution.py:1039
  152.3 2.1 %finish.1 = (f32[64,128]{1,0:T(8,128)}, f32[32,64]{1,0:T(8,128)}, bf16[1,192,1024]{2,1,0:T(8,128)(2,1)}, bf16[1,192,1024]{2,1,0:T(8,128)(2,1)}) custom-call(f32[80,128]{1,0:T(8,128)} %get-tuple-element.11.last, bf16[1,192,1024]{2,1,0:T(8,128)(2,1)} %get-tuple-element.12.out, bf16[1,192,1024]{2,1,0:T(8,128)(2,1)} %get-tuple-element.13.gradient), custom_call_target="tpu_custom_call" | custom-call | tf_op jit(solution)/shard_map/finish/pallas_call | solution.py:1060
